TPU v7x, 256 devices: a whole 4x4x8 slice. The times are simulated.
256 devices in a mesh: section: 16 (over z, core), fsdp: 16 (over y, x).
Axes of the slice: x: 4, y: 4, z: 8, core: 2. Of those that a mesh axis runs over, the one named last changes fastest.
Arguments:
- tokens: bfloat16 [16, 2048, 5120], P('section', 'fsdp'), may hold values from -60 to 60
- cotangents: bfloat16 [16, 2048, 1024], P('section', 'fsdp'), may hold values from -6 to 6
- norm_gain: float32 [16, 5120], P('section'), may hold values from 0.1 to 1.9
- master: float32 [16, 5120, 1024], P('section', 'fsdp'), may hold values from -5 to 5
- moment: float32 [16, 5120, 1024], P('section', 'fsdp'), may hold values from -4 to 4
- second: float32 [16, 5120, 1024], P('section', 'fsdp'), may hold values from 0.05 to 2
- head_owner: int32 [16, 4], P('section'), may hold values from 0 to 3, each once within a row
- plan: int32 [4], replicated, may hold values from 0 to 3, each once
Outputs:
- input_grads: bfloat16 [16, 2048, 5120], P('section', 'fsdp')
- moment_new: float32 [16, 5120, 1024], P('section', 'fsdp')
- second_new: float32 [16, 5120, 1024], P('section', 'fsdp')
- rollout: bfloat16 [16, 1024, 5120], P('section', 'fsdp')
Inputs may be any that keep to these rules, and one draw needn't show every extreme that they name: `head_owner`: each row lists every head once. `plan`: every slot is named once.
All inputs are finite; a program needn't handle non-finite values.
Results may differ from a plain program's by a relative error of at most 0.011.
Values may be sent and summed in bfloat16 or wider, within the bound.
A program may use at most 192 MiB of HBM per device.

v0:
```python
import jax
import jax.numpy as jnp
from jax import lax
from jax.sharding import PartitionSpec as P

beta_one = 0.9
beta_two = 0.95
bias_one = 1.0 - 0.9**10
bias_two = 1.0 - 0.95**10
adam_eps = 1e-08
learn_rate = 0.02
weight_decay = 0.1
norm_eps = 1e-06


def entering(x, axis, join, neutral):
    count = lax.axis_size(axis)
    place = lax.axis_index(axis)
    ahead = count - 1 - place
    gathered = lax.all_gather(x.astype(jnp.bfloat16), axis)
    state = jnp.zeros_like(x) + jnp.asarray(neutral, x.dtype)

    def one(lap, state):
        source = count - 1 - lap
        return join(state, lax.dynamic_index_in_dim(gathered, source, 0, False).astype(x.dtype))

    return lax.fori_loop(0, ahead, one, state)


def plan_rows(cot_rows, plan):
    micro_count = plan.shape[0]
    blocks = cot_rows.reshape(micro_count, -1, cot_rows.shape[-1])
    picker = (plan[:, None] == jnp.arange(micro_count, dtype=jnp.int32)[None, :]).astype(
        jnp.bfloat16
    )
    ordered = jnp.einsum("is,smc->imc", picker, blocks, preferred_element_type=jnp.float32)
    return ordered.astype(jnp.bfloat16).reshape(cot_rows.shape)


def input_term(widened, inverse, gain_row, spread):
    scaled = spread * gain_row
    mean_term = jnp.mean(scaled * widened, axis=-1, keepdims=True)
    return inverse * scaled - widened * inverse * inverse * inverse * mean_term


def adam_step(master, moment, second, gradient):
    moment_new = beta_one * moment + (1.0 - beta_one) * gradient
    second_new = beta_two * second + (1.0 - beta_two) * gradient * gradient
    update = moment_new / bias_one / (jnp.sqrt(second_new / bias_two) + adam_eps)
    weights = master - learn_rate * (update + weight_decay * master)
    return (moment_new, second_new, weights)


def arrange(low_rows, owner_row):
    row_count = low_rows.shape[0]
    head_count = owner_row.shape[0]
    by_head = low_rows.reshape(row_count, 2, head_count, -1)
    picker = (owner_row[:, None] == jnp.arange(head_count, dtype=jnp.int32)[None, :]).astype(
        jnp.bfloat16
    )
    placed = jnp.einsum("jh,rphd->rjpd", picker, by_head, preferred_element_type=jnp.float32)
    return placed.astype(jnp.bfloat16).reshape(row_count, -1)


def add_terms(earlier, later):
    return earlier + later


def shards(tokens, cotangents, norm_gain, master, moment, second, head_owner, plan):
    tok_rows = tokens[0]
    gain_row = norm_gain[0]
    master_rows = master[0]
    owner_row = head_owner[0]
    width = tok_rows.shape[1]
    proj_scale = width ** (-0.5)
    ordered = plan_rows(cotangents[0], plan)
    widened = tok_rows.astype(jnp.float32)
    inverse = lax.rsqrt(jnp.mean(widened * widened, axis=-1, keepdims=True) + norm_eps)
    normed = (widened * inverse * gain_row).astype(jnp.bfloat16)
    low_weights = master_rows.astype(jnp.bfloat16)
    spread = (
        jnp.einsum(
            "tc,rc->tr",
            ordered,
            lax.all_gather(low_weights, "fsdp", axis=0, tiled=True),
            preferred_element_type=jnp.float32,
        )
        * proj_scale
    )
    gradient = lax.psum_scatter(
        (
            jnp.einsum("td,tc->dc", normed, ordered, preferred_element_type=jnp.float32)
            * proj_scale
        ).astype(jnp.bfloat16),
        "fsdp",
        scatter_dimension=0,
        tiled=True,
    ).astype(jnp.float32)
    moment_new, second_new, weights = adam_step(master_rows, moment[0], second[0], gradient)
    arranged = arrange(weights.astype(jnp.bfloat16), owner_row)
    rollout = lax.all_to_all(arranged.T, "fsdp", split_axis=0, concat_axis=1, tiled=True)
    own_term = input_term(widened, inverse, gain_row, spread)
    from_above = entering(own_term, "section", add_terms, jnp.zeros_like(own_term))
    input_grads = (own_term + from_above).astype(jnp.bfloat16)
    return (input_grads[None], moment_new[None], second_new[None], rollout[None])


def solution(mesh):
    in_specs = (
        P("section", "fsdp", None),
        P("section", "fsdp", None),
        P("section", None),
        P("section", "fsdp", None),
        P("section", "fsdp", None),
        P("section", "fsdp", None),
        P("section", None),
        P(),
    )
    out_specs = (
        P("section", "fsdp", None),
        P("section", "fsdp", None),
        P("section", "fsdp", None),
        P("section", "fsdp", None),
    )
    return jax.shard_map(shards, mesh=mesh, in_specs=in_specs, out_specs=out_specs, check_vma=False)
```

profile of v0, /device:TPU:1, one launch (start us, length us, event | category | flops | bytes accessed | tf_op | source)
XLA Modules:
  0.0 363.8 jit_solution(1074620809286612758)
XLA Ops:
  7.2 0.0 copy-start
  7.2 0.0 copy-start.5
  7.2 0.0 copy-start.3
  7.2 0.0 all-gather.4.cloned.1.call-start
  7.2 2.3 bitcast_convert_fusion
  9.5 0.0 all-gather.4.cloned.1.call-update
  9.6 0.0 reduce-scatter.2.cloned.1.call-start
  9.6 0.0 copy-done
  9.6 0.0 copy-done.5
  9.6 0.4 convolution_convert_fusion.1
  10.0 0.1 copy.18
  10.1 0.0 copy-done.3
  10.1 90.2 %all-gather.4.cloned.1.call-done = bf16[5120,1024]{1,0:T(8,128)(2,1)} async-done(((bf16[320,1024]{1,0:T(8,128)(2,1)}), bf16[5120,1024]{1,0:T(8,128)(2,1)}) %all-gather.4.cloned.1.call-update) | async-done | bytes 10485776 | tf_op jit(solution)/shard_map/all_gather | solution.py:85
  100.3 0.0 copy-start.2
  100.3 8.1 %fusion.3 = (f32[128]{0:T(128)S(1)}, f32[128]{0:T(128)S(1)}, f32[128,5120]{1,0:T(8,128)S(1)}) fusion(bf16[1,128,5120]{2,1,0:T(8,128)(2,1)} %param.10, f32[5120]{0:T(1024)S(1)} %broadcast_multiply_fusion, bf16[128,1024]{1,0:T(8,128)(2,1)S(1)} %bitcast.88, bf16[5120,1024]{1,0:T(8,128)(2,1)} %all-gather.4.cloned.1.call-done), kind=kOutput, calls=%fused_computation.8 | convolution fusion | flops 1346109184 | bytes 14701568 | tf_op jit(solution)/shard_map/tc,rc->tr/dot_general | solution.py:82
  108.4 0.0 copy-start.1
  108.4 0.0 copy-done.2
  108.4 5.7 %multiply_convert_fusion = bf16[5120,1024]{1,0:T(8,128)(2,1)} fusion(bf16[128,1024]{1,0:T(8,128)(2,1)S(1)} %bitcast.89, bf16[1,128,5120]{2,1,0:T(8,128)(2,1)S(1)} %copy-done.2, f32[5120]{0:T(1024)S(1)} %bitcast.91, f32[128]{0:T(128)S(1)} %add_rsqrt_fusion), kind=kOutput, calls=%fused_computation.1 | convolution fusion | flops 1355284480 | bytes 12079616 | tf_op jit(solution)/shard_map/td,tc->dc/dot_general | solution.py:92
  114.1 0.0 reduce-scatter.2.cloned.1.call-update
  114.1 0.0 all-gather.6.cloned.1.call-start
  114.2 0.0 copy-done.1
  114.2 3.1 fusion.31
  117.3 0.0 all-gather.6.cloned.1.call-update
  117.3 0.0 copy-start.4
  117.3 90.6 %reduce-scatter.2.cloned.1.call-done = bf16[320,1024]{1,0:T(8,128)(2,1)} async-done(((bf16[5120,1024]{1,0:T(8,128)(2,1)}), bf16[320,1024]{1,0:T(8,128)(2,1)}) %reduce-scatter.2.cloned.1.call-update) | async-done | bytes 655376 | tf_op jit(solution)/shard_map/reduce_scatter | solution.py:90
  207.9 4.9 %fusion.18 = (bf16[320,1024]{1,0:T(8,128)(2,1)S(1)}, f32[1,320,1024]{2,1,0:T(8,128)}, f32[1,320,1024]{2,1,0:T(8,128)}) fusion(f32[1,320,1024]{2,1,0:T(8,128)} %param.13, bf16[320,1024]{1,0:T(8,128)(2,1)} %reduce-scatter.2.cloned.1.call-done, f32[1,320,1024]{2,1,0:T(8,128)} %param.14, f32[1,320,1024]{2,1,0:T(8,128)} %param.15), kind=kLoop, calls=%fused_computation.29 | loop fusion | flops 5570560 | bytes 7864320 | tf_op jit(solution)/shard_map/convert_element_type | solution.py:100
  212.7 0.5 reshape.58
  213.2 0.0 copy-done.4
  213.2 0.6 fusion.21
  213.8 0.7 copy.19
  214.5 0.5 reshape.59
  214.9 1.2 copy.20
  216.1 4.2 %all-to-all-start = ((bf16[16,64,320]{2,1,0:T(8,128)(2,1)}), bf16[16,64,320]{2,1,0:T(8,128)(2,1)S(1)}, u32[]{:S(2)}, u32[]{:S(2)}) async-start(bf16[16,64,320]{2,1,0:T(8,128)(2,1)} %bitcast.19), calls=%async_computation.1 | async-start | bytes 1572864 | tf_op jit(solution)/shard_map/all_to_all | solution.py:101
  220.3 12.3 %all-to-all-done = bf16[16,64,320]{2,1,0:T(8,128)(2,1)S(1)} async-done(((bf16[16,64,320]{2,1,0:T(8,128)(2,1)}), bf16[16,64,320]{2,1,0:T(8,128)(2,1)S(1)}, u32[]{:S(2)}, u32[]{:S(2)}) %all-to-all-start) | async-done | bytes 655392 | tf_op jit(solution)/shard_map/all_to_all | solution.py:101
  232.7 0.5 copy.21
  233.1 1.5 broadcast_in_dim.24
  234.6 91.4 %all-gather.6.cloned.1.call-done = bf16[2048,5120]{1,0:T(8,128)(2,1)} async-done(((bf16[128,5120]{1,0:T(8,128)(2,1)}), bf16[2048,5120]{1,0:T(8,128)(2,1)}) %all-gather.6.cloned.1.call-update) | async-done | bytes 20971536 | tf_op jit(solution)/shard_map/all_gather | solution.py:20
  326.1 0.2 broadcast_in_dim.20
  326.3 26.9 %while.12 = (s32[]{:T(128)}, f32[128,5120]{1,0:T(8,128)S(1)}, s32[]{:T(128)}, bf16[16,128,5120]{2,1,0:T(8,128)(2,1)}, s32[]{:T(128)}, /*index=5*/s32[]{:T(128)}, s32[]{:T(128)}, s32[]{:T(128)}) while((s32[]{:T(128)}, f32[128,5120]{1,0:T(8,128)S(1)}, s32[]{:T(128)}, bf16[16,128,5120]{2,1,0:T(8,128)(2,1)}, s32[]{:T(128)}, /*index=5*/s32[]{:T(128)}, ...), condition=%wide.region_3.4_spmd, body=%wide.region_2.0_spmd.sunk | while | flops 1310726 | bytes 6553743 | solution.py:27
  326.3 1.9 convert_add_fusion.2
  328.3 1.9 convert_add_fusion.2
  330.2 1.9 convert_add_fusion.2
  332.1 1.9 convert_add_fusion.2
  334.0 1.9 convert_add_fusion.2
  336.0 1.9 convert_add_fusion.2
  337.9 1.9 convert_add_fusion.2
  339.8 1.9 convert_add_fusion.2
  341.7 1.9 convert_add_fusion.2
  343.6 1.9 convert_add_fusion.2
  345.6 1.9 convert_add_fusion.2
  347.5 1.9 convert_add_fusion.2
  349.4 1.9 convert_add_fusion.2
  351.3 1.9 convert_add_fusion.2
  353.3 4.0 %fusion.13 = bf16[1,128,5120]{2,1,0:T(8,128)(2,1)} fusion(f32[128,5120]{1,0:T(8,128)S(1)} %get-tuple-element.60, f32[128]{0:T(128)S(1)} %broadcast_multiply_fusion.1, bf16[1,128,5120]{2,1,0:T(8,128)(2,1)} %param.10, f32[128,5120]{1,0:T(8,128)} %copy-done.1, f32[128]{0:T(128)S(1)} %add_rsqrt_fusion), kind=kLoop, calls=%fused_computation.22 | loop fusion | flops 5898240 | bytes 7865344 | tf_op jit(solution)/shard_map/broadcast_in_dim | solution.py:105
  (3 shorter events, 0.0 us)
Async XLA Ops:
  7.2 2.4 copy-start
  7.2 2.4 copy-start.5
  7.2 2.9 copy-start.3
  7.2 93.1 %all-gather.4.cloned.1.call-start = ((), (), s32[]{:S(2)}) async-start(), calls=%async_computation.2 | async-start | bytes 11141120 | tf_op jit(solution)/shard_map/all_gather | solution.py:85
  9.6 198.3 %reduce-scatter.2.cloned.1.call-start = ((), (), s32[]{:S(2)}) async-start(), calls=%async_computation.3 | async-start | bytes 11141120 | tf_op jit(solution)/shard_map/reduce_scatter | solution.py:90
  100.3 8.1 %copy-start.2 = (bf16[1,128,5120]{2,1,0:T(8,128)(2,1)S(1)}, bf16[1,128,5120]{2,1,0:T(8,128)(2,1)}, u32[]{:S(2)}) copy-start(bf16[1,128,5120]{2,1,0:T(8,128)(2,1)} %param.10) | copy-start | bytes 3932164
  108.4 5.8 %copy-start.1 = (f32[128,5120]{1,0:T(8,128)}, f32[128,5120]{1,0:T(8,128)S(1)}, u32[]{:S(2)}) copy-start(f32[128,5120]{1,0:T(8,128)S(1)} %get-tuple-element.74) | copy-start | bytes 7864324
  114.1 211.9 %all-gather.6.cloned.1.call-start = ((), (), s32[]{:S(2)}) async-start(), calls=%async_computation.4 | async-start | bytes 22282240 | tf_op jit(solution)/shard_map/all_gather | solution.py:20
  117.3 95.9 %copy-start.4 = (s32[1,4]{1,0:T(1,128)S(1)}, s32[1,4]{1,0:T(1,128)}, u32[]{:S(2)}) copy-start(s32[1,4]{1,0:T(1,128)} %param.16) | copy-start | bytes 52
  216.1 16.6 %all-to-all-start = ((bf16[16,64,320]{2,1,0:T(8,128)(2,1)}), bf16[16,64,320]{2,1,0:T(8,128)(2,1)S(1)}, u32[]{:S(2)}, u32[]{:S(2)}) async-start(bf16[16,64,320]{2,1,0:T(8,128)(2,1)} %bitcast.19), calls=%async_computation.1 | async-start | bytes 1572864 | tf_op jit(solution)/shard_map/all_to_all | solution.py:101
Sparse Core Ops, SparseCore 0:
  11.0 89.1 all-gather.3
  114.3 93.5 reduce-scatter.1
  210.3 115.7 all-gather.5
where the time goes:
time: 365 us; the launch traced here: 364 us
  waiting for transfers between devices  285 us (78%)
  other arithmetic  40.9 us (11%)
  matrix products  14.7 us (4%)
  between operations  13.9 us (4%)
  local copies, waits for them, and re-layouts  5.05 us (1%)
  starting transfers between devices  4.37 us (1%)
    all_gather x1, waiting for transfers between devices, entering(): gathered = lax.all_gather(x.astype(jnp.bfloat16), axis)  91.4 us
    reduce_scatter x1, waiting for transfers between devices, shards(): lax.psum_scatter((jnp.einsum('td,tc->dc', normed, ordered, preferred_elem...  90.6 us
    all_gather x1, waiting for transfers between devices, shards(): lax.all_gather(low_weights, 'fsdp', axis=0, tiled=True)  90.2 us
    add x14, other arithmetic, add_terms(): return earlier + later  26.6 us
    all_to_all x1, waiting for transfers between devices, shards(): lax.all_to_all(arranged.T, 'fsdp', split_axis=0, concat_axis=1, tiled=True)  12.3 us
    dot_general x1, matrix products, shards(): jnp.einsum('tc,rc->tr', ordered, lax.all_gather(low_weights, 'fsdp', axis...  8.09 us
  transfers between devices with their start and end apart: 4, of which 4 were waited for; matrix products, arithmetic and copies ran while one was open for 4% of the time, Pallas kernels for 0%

commit v1 on v0

v1 whole, which is shorter than its diff:
```python
import functools

import jax
import jax.numpy as jnp
from jax import lax
from jax.experimental import pallas as pl
from jax.experimental.pallas import tpu as pltpu
from jax.sharding import PartitionSpec as P

beta_one = 0.9
beta_two = 0.95
bias_one = 1.0 - 0.9**10
bias_two = 1.0 - 0.95**10
adam_eps = 1e-08
learn_rate = 0.02
weight_decay = 0.1
norm_eps = 1e-06

MESH = pl.DeviceIdType.MESH
F32 = jnp.float32
BF16 = jnp.bfloat16

D = 5120
C = 1024
T = 128
R = 320
H = R // 2
QD = D // 4
HD = D // 2
MB = 32
NMB = 4
CH = 16
NCH = T // CH
RO = 64


def kernel(
    tok_hbm, cot_hbm, gain, mas_hbm, mom_hbm, sec_hbm, owner, plan,
    ig_hbm, mn_hbm, sn_hbm, ro_hbm,
    tok, cot, mas, mom, sec,
    wg, g, xs, xr, ss, sr, inv,
    pf, s_opp, s_right, s_left, o_left, o_right, r_left, r_right,
    wnew, rs, rr, ro,
    own, es, er, us, ur, mr, out,
    in_sem, out_sem, og_sem,
    w_ss, w_rs, g_ss, g_rs, x_ss, x_rs, s_ss, s_rs, p_ss, p_rs, r_ss, r_rs,
    e_ss, e_rs, u_ss, u_rs, m_ss, m_rs,
):
    s = lax.axis_index("section")
    f = lax.axis_index("fsdp")
    z, c = s // 2, s % 2
    y, x = f // 4, f % 4

    def at_x(d):
        return (s, y * 4 + lax.rem(x + d, 4))

    def at_y(d):
        return (s, lax.rem(y + d, 4) * 4 + x)

    partner = (z * 2 + 1 - c, f)
    below = (lax.rem(z + 7, 8) * 2 + c, f)
    above = (lax.rem(z + 1, 8) * 2 + c, f)

    def send(src, dst, ssem, rsem, dev):
        return pltpu.make_async_remote_copy(
            src_ref=src, dst_ref=dst, send_sem=ssem, recv_sem=rsem, device_id=dev, device_id_type=MESH
        )

    loads = [
        pltpu.make_async_copy(a, b, in_sem.at[i])
        for i, (a, b) in enumerate(
            [(mas_hbm, mas), (cot_hbm, cot), (tok_hbm, tok), (mom_hbm, mom), (sec_hbm, sec)]
        )
    ]
    for ld in loads:
        ld.start()

    bar = pltpu.get_barrier_semaphore()
    for k in range(1, 16):
        pl.semaphore_signal(bar, inc=1, device_id=(s, lax.rem(f + k, 16)), device_id_type=MESH)
    for dev in (partner, below, above):
        pl.semaphore_signal(bar, inc=1, device_id=dev, device_id_type=MESH)

    @pl.when(z == 7)
    def _():
        ur[...] = jnp.zeros_like(ur)

    def w_rows(block, half):
        return pl.ds(pl.multiple_of(block * R + half * H, 32), H)

    loads[0].wait()
    wg[pl.ds(pl.multiple_of(x * R, 32), R), :] = mas[...].astype(BF16)

    loads[1].wait()
    for i in range(NMB):
        p = plan[i]
        v = cot[0:MB, :]
        for j in range(1, NMB):
            v = jnp.where(p == j, cot[j * MB : (j + 1) * MB, :], v)
        g[0, i * MB : (i + 1) * MB, :] = v

    pl.semaphore_wait(bar, 18)

    w_out = []
    for n, (dev, half) in enumerate([(1, 0), (3, 1), (1, 1), (3, 0)]):
        rows = w_rows(x, half)
        w_out.append(send(wg.at[rows], wg.at[rows], w_ss.at[n], w_rs.at[n], at_x(dev)))
    for cp in w_out:
        cp.start()

    g_out = []
    hg = T // 2
    for n, (dev, half) in enumerate([(1, 0), (3, 1), (1, 1), (3, 0)]):
        rows = pl.ds(half * hg, hg)
        g_out.append(send(g.at[0, rows], g.at[dev, rows], g_ss.at[n], g_rs.at[n], at_y(dev)))
    for cp in g_out:
        cp.start()

    loads[2].wait()

    def norm_chunk(k, carry):
        rows = pl.ds(pl.multiple_of(k * CH, CH), CH)
        acc = jnp.zeros((CH, 1), F32)
        for b in range(4):
            v = tok[rows, b * QD : (b + 1) * QD].astype(F32)
            acc = acc + jnp.sum(v * v, axis=-1, keepdims=True)
        iv = lax.rsqrt(acc * (1.0 / D) + norm_eps)
        inv[rows, :] = jnp.broadcast_to(iv, (CH, 128))
        for b in range(4):
            v = tok[rows, b * QD : (b + 1) * QD].astype(F32)
            xs[b, rows, :] = (v * iv * gain[:, b * QD : (b + 1) * QD]).astype(BF16)
        return carry

    lax.fori_loop(0, NCH, norm_chunk, 0)

    x_out = []
    for n, dev in enumerate([2, 1, 3]):
        x_out.append(
            send(xs.at[lax.rem(y + dev, 4)], xr.at[dev], x_ss.at[n], x_rs.at[n], at_y(dev))
        )
    for cp in x_out:
        cp.start()
    xr[0] = xs[y]

    g_out[0].wait_recv()
    rows0, rows1 = pl.ds(0, hg), pl.ds(hg, hg)
    g_fwd = [send(g.at[1, rows0], g.at[2, rows0], g_ss.at[4], g_rs.at[4], at_y(1))]
    g_fwd[0].start()
    g_out[1].wait_recv()
    g_fwd.append(send(g.at[3, rows1], g.at[2, rows1], g_ss.at[5], g_rs.at[5], at_y(3)))
    g_fwd[1].start()

    w_out[0].wait_recv()
    rows = w_rows(lax.rem(x + 3, 4), 0)
    w_fwd = [send(wg.at[rows], wg.at[rows], w_ss.at[4], w_rs.at[4], at_x(1))]
    w_fwd[0].start()
    w_out[1].wait_recv()
    rows = w_rows(lax.rem(x + 1, 4), 1)
    w_fwd.append(send(wg.at[rows], wg.at[rows], w_ss.at[5], w_rs.at[5], at_x(3)))
    w_fwd[1].start()

    for cp in (g_out[2], g_out[3], g_fwd[0], g_fwd[1]):
        cp.wait_recv()
    for cp in (w_out[2], w_out[3], w_fwd[0], w_fwd[1]):
        cp.wait_recv()

    proj_scale = D ** (-0.5)
    sr_out = []

    for i in range(NMB):
        rows = pl.ds(i * MB, MB)
        lhs = jnp.concatenate([g[r, i * MB : (i + 1) * MB, :] for r in range(4)], axis=0)
        for q in range(5):
            cols = slice(q * 256, (q + 1) * 256)
            v = (
                lax.dot_general(
                    lhs, wg[q * 256 : (q + 1) * 256, :], (((1,), (1,)), ((), ())),
                    preferred_element_type=F32,
                )
                * proj_scale
            ).astype(BF16)
            for r in range(1, 4):
                ss[r, i * MB : (i + 1) * MB, cols] = v[r * MB : (r + 1) * MB]
            sr[y, i * MB : (i + 1) * MB, cols] = v[0:MB]
        for n, r in enumerate([2, 1, 3]):
            cp = send(ss.at[r, rows], sr.at[y, rows], s_ss.at[i, n], s_rs.at[i, n], at_y(4 - r))
            cp.start()
            sr_out.append(cp)

    for cp in x_out:
        cp.wait_recv()
    gall = g[...].reshape(4 * T, C)
    for q in range(5):
        lhs = jnp.concatenate([xr[r, :, q * 256 : (q + 1) * 256] for r in range(4)], axis=0)
        pf[q * 256 : (q + 1) * 256, :] = (
            lax.dot_general(lhs, gall, (((0,), (0,)), ((), ())), preferred_element_type=F32)
            * proj_scale
        )

    def p_rows(d, half):
        return pf[pl.ds(pl.multiple_of(lax.rem(x + d, 4) * R + half * H, 32), H), :]

    s_opp[0:H, :] = p_rows(2, 0).astype(BF16)
    s_opp[H:R, :] = p_rows(2, 1).astype(BF16)
    p_out = [
        send(s_opp.at[pl.ds(0, H)], o_left, p_ss.at[0], p_rs.at[0], at_x(1)),
        send(s_opp.at[pl.ds(H, H)], o_right, p_ss.at[1], p_rs.at[1], at_x(3)),
    ]
    for cp in p_out:
        cp.start()
    s_right[H:R, :] = p_rows(1, 1).astype(BF16)
    s_left[0:H, :] = p_rows(3, 0).astype(BF16)
    p_out += [
        send(s_right.at[pl.ds(H, H)], r_left.at[pl.ds(H, H)], p_ss.at[2], p_rs.at[2], at_x(1)),
        send(s_left.at[pl.ds(0, H)], r_right.at[pl.ds(0, H)], p_ss.at[3], p_rs.at[3], at_x(3)),
    ]
    for cp in p_out[2:]:
        cp.start()
    p_out += [
        send(s_right.at[pl.ds(0, H)], r_left.at[pl.ds(0, H)], p_ss.at[4], p_rs.at[4], at_x(1)),
        send(s_left.at[pl.ds(H, H)], r_right.at[pl.ds(H, H)], p_ss.at[5], p_rs.at[5], at_x(3)),
    ]

    def reduce_forward():
        p_out[0].wait_recv()
        s_right[0:H, :] = (p_rows(1, 0) + o_left[...].astype(F32)).astype(BF16)
        p_out[4].start()
        p_out[1].wait_recv()
        s_left[H:R, :] = (p_rows(3, 1) + o_right[...].astype(F32)).astype(BF16)
        p_out[5].start()

    mn_copy = pltpu.make_async_copy(mom, mn_hbm, out_sem.at[0])
    sn_copy = pltpu.make_async_copy(sec, sn_hbm, out_sem.at[1])
    ro_copy = pltpu.make_async_copy(ro, ro_hbm, out_sem.at[2])

    r_out = [
        send(
            rs.at[lax.rem(f + k, 16)], rr.at[f], r_ss.at[k - 1], r_rs.at[k - 1],
            (s, lax.rem(f + k, 16)),
        )
        for k in range(1, 16)
    ]

    def update():
        for cp in p_out[2:]:
            cp.wait_recv()
        loads[3].wait()
        loads[4].wait()

        def adam(k, carry):
            rows = pl.ds(pl.multiple_of(k * 32, 32), 32)
            grad = (
                pf[pl.ds(pl.multiple_of(x * R + k * 32, 32), 32), :]
                + r_left[rows, :].astype(F32)
                + r_right[rows, :].astype(F32)
            )
            m = beta_one * mom[rows, :] + (1.0 - beta_one) * grad
            v = beta_two * sec[rows, :] + (1.0 - beta_two) * grad * grad
            mom[rows, :] = m
            sec[rows, :] = v
            step = m * (1.0 / bias_one) / (jnp.sqrt(v * (1.0 / bias_two)) + adam_eps)
            old = mas[rows, :]
            wnew[rows, :] = (old - learn_rate * (step + weight_decay * old)).astype(BF16)
            return carry

        lax.fori_loop(0, R // 32, adam, 0)
        mn_copy.start()
        sn_copy.start()

        ia = lax.broadcasted_iota(jnp.int32, (128, 128), 0)
        ib = lax.broadcasted_iota(jnp.int32, (128, 128), 1)
        eye = jnp.where(ia == ib, 1.0, 0.0).astype(BF16)
        for j in range(4):
            o = owner[j]
            for p in range(2):
                v = wnew[:, p * 512 : p * 512 + 128]
                for h in range(1, 4):
                    v = jnp.where(o == h, wnew[:, p * 512 + h * 128 : p * 512 + (h + 1) * 128], v)
                t = lax.dot_general(
                    eye, v, (((1,), (1,)), ((), ())), preferred_element_type=F32
                ).astype(BF16)
                rs[j * 4 + p * 2] = t[0:RO]
                rs[j * 4 + p * 2 + 1] = t[RO : 2 * RO]
        for cp in r_out:
            cp.start()
        rr[f] = rs[f]

    def chain_rows(k):
        return pl.ds(pl.multiple_of(k * CH, CH), CH)

    def e_copy(k):
        rows = chain_rows(k)
        return send(es.at[:, rows], er.at[:, rows], e_ss.at[k], e_rs.at[k], partner)

    def u_copy(k, q):
        rows = chain_rows(k)
        return send(us.at[q, rows], ur.at[q, rows], u_ss.at[k, q], u_rs.at[k, q], below)

    def m_copy(k, q, ref):
        rows = chain_rows(k)
        return send(ref.at[q, rows], mr.at[q, rows], m_ss.at[k, q], m_rs.at[k, q], partner)

    def og_copy(k):
        rows = chain_rows(k)
        return [
            pltpu.make_async_copy(
                out.at[b, rows], ig_hbm.at[rows, pl.ds(b * QD, QD)], og_sem.at[k, b]
            )
            for b in range(4)
        ]

    def finish(k):
        rows = chain_rows(k)
        for q in range(2):
            m_copy(k, q, us).wait_recv()
            b = (1 - c) * 2 + q
            m = mr[q, rows, :].astype(F32)
            out[b, rows, :] = jnp.where(c == 1, m + own[b, rows, :], m).astype(BF16)
        for cp in og_copy(k):
            cp.start()

    def chain_step(k, first):
        rows = chain_rows(k)
        acc = jnp.zeros((CH, 1), F32)
        for b in range(4):
            t = tok[rows, b * QD : (b + 1) * QD].astype(F32)
            sc = sr[b, rows, :].astype(F32) * gain[:, b * QD : (b + 1) * QD]
            acc = acc + jnp.sum(sc * t, axis=-1, keepdims=True)
        iv = inv[rows, 0:1]
        coef = iv * iv * iv * (acc * (1.0 / D))
        for b in range(4):
            t = tok[rows, b * QD : (b + 1) * QD].astype(F32)
            sc = sr[b, rows, :].astype(F32) * gain[:, b * QD : (b + 1) * QD]
            own[b, rows, :] = iv * sc - t * coef
        for q in range(2):
            es[q, rows, :] = own[(1 - c) * 2 + q, rows, :].astype(BF16)
        e_copy(k).start()
        e_copy(k).wait_recv()
        for q in range(2):

            @pl.when(z < 7)
            def _():
                u_copy(k, q).wait_recv()

            b = c * 2 + q
            u = ur[q, rows, :].astype(F32)
            mine = u + own[b, rows, :]
            un = mine + er[q, rows, :].astype(F32)
            unb = un.astype(BF16)
            us[q, rows, :] = unb

            @pl.when(z > 0)
            def _():
                u_copy(k, q).start()

            @pl.when(c == 0)
            def _():
                m_copy(k, q, ur).start()

            @pl.when(c == 1)
            def _():
                m_copy(k, q, us).start()

            out[b, rows, :] = jnp.where(c == 1, mine.astype(BF16), unb)

        if not first:
            finish(k - 1)

    fwd_slot = jnp.where(z == 7, 1, 0)
    upd_slot = jnp.minimum(z, 4)

    for i in range(NMB + 1):

        @pl.when(fwd_slot == i)
        def _():
            reduce_forward()

        @pl.when(upd_slot == i)
        def _():
            update()

        if i < NMB:
            for n in range(3):
                sr_out[i * 3 + n].wait_recv()
            for h in range(MB // CH):
                k = i * (MB // CH) + h
                chain_step(k, k == 0)
    finish(NCH - 1)

    for cp in r_out:
        cp.wait_recv()
    for i in range(8):
        ro[:, i * 2 * R : (i + 1) * 2 * R] = jnp.concatenate([rr[2 * i], rr[2 * i + 1]], axis=1)
    ro_copy.start()

    for cp in w_out + w_fwd + g_out + g_fwd + x_out + sr_out + p_out + r_out:
        cp.wait_send()

    def drain(k, carry):
        e_copy(k).wait_send()
        for q in range(2):
            m_copy(k, q, us).wait_send()

            @pl.when(z > 0)
            def _():
                u_copy(k, q).wait_send()

        for cp in og_copy(k):
            cp.wait()
        return carry

    lax.fori_loop(0, NCH, drain, 0)
    mn_copy.wait()
    sn_copy.wait()
    ro_copy.wait()


def shards(tokens, cotangents, norm_gain, master, moment, second, head_owner, plan):
    hbm = pl.BlockSpec(memory_space=pl.ANY)
    vmem = pl.BlockSpec(memory_space=pltpu.VMEM)
    smem = pl.BlockSpec(memory_space=pltpu.SMEM)
    V = pltpu.VMEM
    dma = pltpu.SemaphoreType.DMA
    scratch = [
        V((T, D), BF16), V((T, C), BF16), V((R, C), F32), V((R, C), F32), V((R, C), F32),
        V((4 * R, C), BF16), V((4, T, C), BF16), V((4, T, QD), BF16), V((4, T, QD), BF16),
        V((4, T, QD), BF16), V((4, T, QD), BF16), V((T, 128), F32),
        V((4 * R, C), F32), V((R, C), BF16), V((R, C), BF16), V((R, C), BF16),
        V((H, C), BF16), V((H, C), BF16), V((R, C), BF16), V((R, C), BF16),
        V((R, C), BF16), V((16, RO, R), BF16), V((16, RO, R), BF16), V((RO, D), BF16),
        V((4, T, QD), F32), V((2, T, QD), BF16), V((2, T, QD), BF16), V((2, T, QD), BF16),
        V((2, T, QD), BF16), V((2, T, QD), BF16), V((4, T, QD), BF16),
        dma((5,)), dma((3,)), dma((NCH, 4)),
        dma((6,)), dma((6,)), dma((6,)), dma((6,)), dma((3,)), dma((3,)),
        dma((NMB, 3)), dma((NMB, 3)), dma((6,)), dma((6,)), dma((15,)), dma((15,)),
        dma((NCH,)), dma((NCH,)), dma((NCH, 2)), dma((NCH, 2)), dma((NCH, 2)), dma((NCH, 2)),
    ]
    ig, mn, sn, ro = pl.pallas_call(
        kernel,
        out_shape=(
            jax.ShapeDtypeStruct((T, D), BF16),
            jax.ShapeDtypeStruct((R, C), F32),
            jax.ShapeDtypeStruct((R, C), F32),
            jax.ShapeDtypeStruct((RO, D), BF16),
        ),
        in_specs=[hbm, hbm, vmem, hbm, hbm, hbm, smem, smem],
        out_specs=(hbm, hbm, hbm, hbm),
        scratch_shapes=scratch,
        name="layer_backward",
        cost_estimate=pl.CostEstimate(
            flops=4 * T * C * D, bytes_accessed=12_000_000, transcendentals=2 * R * C
        ),
        compiler_params=pltpu.CompilerParams(
            collective_id=0, has_side_effects=True, vmem_limit_bytes=56 * 1024 * 1024
        ),
    )(tokens[0], cotangents[0], norm_gain, master[0], moment[0], second[0], head_owner[0], plan)
    return (ig[None], mn[None], sn[None], ro[None])


def solution(mesh):
    in_specs = (
        P("section", "fsdp", None),
        P("section", "fsdp", None),
        P("section", None),
        P("section", "fsdp", None),
        P("section", "fsdp", None),
        P("section", "fsdp", None),
        P("section", None),
        P(),
    )
    out_specs = (
        P("section", "fsdp", None),
        P("section", "fsdp", None),
        P("section", "fsdp", None),
        P("section", "fsdp", None),
    )
    return jax.shard_map(shards, mesh=mesh, in_specs=in_specs, out_specs=out_specs, check_vma=False)
```

time: 365 us -> 101 us (0.28)
  waiting for transfers between devices: 285 us -> 0 us
  Pallas kernels: 0 us -> 93 us
  other arithmetic: 40.9 us -> 0 us
  matrix products: 14.7 us -> 0 us
  between operations: 13.9 us -> 0.65 us
  starting transfers between devices: 4.37 us -> 0 us
    all_gather x2 -> x0, waiting for transfers between devices: 182 us -> none  [the longest x1 91.4 us: entering(): gathered = lax.all_gather(x.astype(jnp.bfloat16), axis)]
    pallas_call x0 -> x1, Pallas kernels: none -> 93 us  [shards(): pl.pallas_call(kernel, out_shape=(jax.ShapeDtypeStruct((T, D), BF16), jax...]
    reduce_scatter x1 -> x0, waiting for transfers between devices: 90.6 us -> none  [shards(): lax.psum_scatter((jnp.einsum('td,tc->dc', normed, ordered, preferred_elem...]
    add x14 -> x0, other arithmetic: 26.6 us -> none  [add_terms(): return earlier + later]
    dot_general x4 -> x0, matrix products: 14.7 us -> none  [the longest x1 8.09 us: shards(): jnp.einsum('tc,rc->tr', ordered, lax.all_gather(low_weights, 'fsdp', axis...]
    all_to_all x1 -> x0, waiting for transfers between devices: 12.3 us -> none  [shards(): lax.all_to_all(arranged.T, 'fsdp', split_axis=0, concat_axis=1, tiled=True)]
    convert_element_type x3 -> x0, other arithmetic: 10.2 us -> none  [the longest x1 4.86 us: shards(): arranged = arrange(weights.astype(jnp.bfloat16), owner_row)]
    unnamed x12 -> x10, local copies, waits for them, and re-layouts: 0.03 us -> 6.72 us
  transfers between devices with their start and end apart: 4 -> 0, of which waited for: 4 -> 0; matrix products, arithmetic and copies ran while one was open for 4% -> 0% of each run, Pallas kernels for 0% -> 0%
where the time goes in v1:
time: 101 us; the launch traced here: 100 us
  Pallas kernels  93 us (92%)
  local copies, waits for them, and re-layouts  6.72 us (7%)
    pallas_call x1, Pallas kernels, shards(): pl.pallas_call(kernel, out_shape=(jax.ShapeDtypeStruct((T, D), BF16), jax...  93 us
    unnamed x10, local copies, waits for them, and re-layouts  6.72 us

profile of v1, /device:TPU:1, one launch (start us, length us, event | category | flops | bytes accessed | tf_op | source)
XLA Modules:
  0.0 100.3 jit_solution(16031237362994134363)
XLA Ops:
  0.6 93.0 %layer_backward.1 = (bf16[128,5120]{1,0:T(8,128)(2,1)}, f32[320,1024]{1,0:T(8,128)}, f32[320,1024]{1,0:T(8,128)}, bf16[64,5120]{1,0:T(8,128)(2,1)}) custom-call(bf16[128,5120]{1,0:T(8,128)(2,1)} %bitcast.14, bf16[128,1024]{1,0:T(8,128)(2,1)} %bitcast.18, f32[1,5120]{1,0:T(1,128)} %gain.1, f32[320,1024]{1,0:T(8,128)} %bitcast.15, f32[320,1024]{1,0:T(8,128)} %bitcast.16, ...), custom_call_target="tpu_custom_call" | custom-call | flops 2684354560 | bytes 12000000 | tf_op jit(solution)/shard_map/layer_backward/pallas_call | solution.py:438
  93.6 0.0 copy-start.1
  93.6 2.6 %copy.16 = bf16[1,128,5120]{2,1,0:T(8,128)(2,1)} copy(bf16[1,128,5120]{2,1,0:T(8,128)(2,1)} %bitcast.12) | data formatting | bytes 2621440
  96.2 0.0 copy-done.1
  96.2 0.0 copy-start
  96.2 1.1 %copy.17 = f32[1,320,1024]{2,1,0:T(8,128)} copy(f32[1,320,1024]{2,1,0:T(8,128)S(1)} %bitcast.11) | data formatting | bytes 2621440
  97.2 0.7 copy-done
  98.0 0.0 copy-start.2
  98.0 1.1 %copy.18 = f32[1,320,1024]{2,1,0:T(8,128)} copy(f32[1,320,1024]{2,1,0:T(8,128)S(1)} %bitcast.10) | data formatting | bytes 2621440
  99.0 0.5 copy-done.2
  99.5 0.8 copy.19
Async XLA Ops:
  93.6 2.6 %copy-start.1 = (f32[320,1024]{1,0:T(8,128)S(1)}, f32[320,1024]{1,0:T(8,128)}, u32[]{:S(2)}) copy-start(f32[320,1024]{1,0:T(8,128)} %get-tuple-element.9) | copy-start | bytes 3932164
  96.2 1.8 %copy-start = (f32[320,1024]{1,0:T(8,128)S(1)}, f32[320,1024]{1,0:T(8,128)}, u32[]{:S(2)}) copy-start(f32[320,1024]{1,0:T(8,128)} %get-tuple-element.10) | copy-start | bytes 3932164
  98.0 1.5 %copy-start.2 = (bf16[64,5120]{1,0:T(8,128)(2,1)S(1)}, bf16[64,5120]{1,0:T(8,128)(2,1)}, u32[]{:S(2)}) copy-start(bf16[64,5120]{1,0:T(8,128)(2,1)} %get-tuple-element.11) | copy-start | bytes 1966084

commit v2 on v1

--- a/solution.py
+++ b/solution.py
@@ -31,6 +31,10 @@
 NMB = 4
 CH = 16
 NCH = T // CH
+HOP = 2
+FORWARD_SLOT = 4
+UPDATE_SLOT = 10
+LAND = 1
 RO = 64
 
 
@@ -41,10 +45,10 @@
     wg, g, xs, xr, ss, sr, inv,
     pf, s_opp, s_right, s_left, o_left, o_right, r_left, r_right,
     wnew, rs, rr, ro,
-    own, es, er, us, ur, mr, out,
+    own, es, er, ds, dr, us, ur, ls, lr, ms, mr, out,
     in_sem, out_sem, og_sem,
     w_ss, w_rs, g_ss, g_rs, x_ss, x_rs, s_ss, s_rs, p_ss, p_rs, r_ss, r_rs,
-    e_ss, e_rs, u_ss, u_rs, m_ss, m_rs,
+    e_ss, e_rs, d_ss, d_rs, u_ss, u_rs, l_ss, l_rs, m_ss, m_rs,
 ):
     s = lax.axis_index("section")
     f = lax.axis_index("fsdp")
@@ -81,9 +85,11 @@
     for dev in (partner, below, above):
         pl.semaphore_signal(bar, inc=1, device_id=dev, device_id_type=MESH)
 
-    @pl.when(z == 7)
-    def _():
-        ur[...] = jnp.zeros_like(ur)
+    for top, ref in ((7, dr), (4, ur), (3, lr)):
+
+        @pl.when(z == top)
+        def _():
+            ref[...] = jnp.zeros_like(ref)
 
     def w_rows(block, half):
         return pl.ds(pl.multiple_of(block * R + half * H, 32), H)
@@ -161,31 +167,7 @@
 
     for cp in (g_out[2], g_out[3], g_fwd[0], g_fwd[1]):
         cp.wait_recv()
-    for cp in (w_out[2], w_out[3], w_fwd[0], w_fwd[1]):
-        cp.wait_recv()
-
     proj_scale = D ** (-0.5)
-    sr_out = []
-
-    for i in range(NMB):
-        rows = pl.ds(i * MB, MB)
-        lhs = jnp.concatenate([g[r, i * MB : (i + 1) * MB, :] for r in range(4)], axis=0)
-        for q in range(5):
-            cols = slice(q * 256, (q + 1) * 256)
-            v = (
-                lax.dot_general(
-                    lhs, wg[q * 256 : (q + 1) * 256, :], (((1,), (1,)), ((), ())),
-                    preferred_element_type=F32,
-                )
-                * proj_scale
-            ).astype(BF16)
-            for r in range(1, 4):
-                ss[r, i * MB : (i + 1) * MB, cols] = v[r * MB : (r + 1) * MB]
-            sr[y, i * MB : (i + 1) * MB, cols] = v[0:MB]
-        for n, r in enumerate([2, 1, 3]):
-            cp = send(ss.at[r, rows], sr.at[y, rows], s_ss.at[i, n], s_rs.at[i, n], at_y(4 - r))
-            cp.start()
-            sr_out.append(cp)
 
     for cp in x_out:
         cp.wait_recv()
@@ -221,6 +203,35 @@
         send(s_left.at[pl.ds(H, H)], r_right.at[pl.ds(H, H)], p_ss.at[5], p_rs.at[5], at_x(3)),
     ]
 
+    for cp in (w_out[2], w_out[3], w_fwd[0], w_fwd[1]):
+        cp.wait_recv()
+
+    sr_out = []
+
+    def s_recv(i, n):
+        rows = pl.ds(pl.multiple_of(i * MB, MB), MB)
+        return send(ss.at[0, rows], sr.at[0, rows], s_ss.at[i, n], s_rs.at[i, n], at_y(1))
+
+    for i in range(NMB):
+        rows = pl.ds(i * MB, MB)
+        lhs = jnp.concatenate([g[r, i * MB : (i + 1) * MB, :] for r in range(4)], axis=0)
+        for q in range(5):
+            cols = slice(q * 256, (q + 1) * 256)
+            v = (
+                lax.dot_general(
+                    lhs, wg[q * 256 : (q + 1) * 256, :], (((1,), (1,)), ((), ())),
+                    preferred_element_type=F32,
+                )
+                * proj_scale
+            ).astype(BF16)
+            for r in range(1, 4):
+                ss[r, i * MB : (i + 1) * MB, cols] = v[r * MB : (r + 1) * MB]
+            sr[y, i * MB : (i + 1) * MB, cols] = v[0:MB]
+        for n, r in enumerate([2, 1, 3]):
+            cp = send(ss.at[r, rows], sr.at[y, rows], s_ss.at[i, n], s_rs.at[i, n], at_y(4 - r))
+            cp.start()
+            sr_out.append(cp)
+
     def reduce_forward():
         p_out[0].wait_recv()
         s_right[0:H, :] = (p_rows(1, 0) + o_left[...].astype(F32)).astype(BF16)
@@ -292,13 +303,24 @@
         rows = chain_rows(k)
         return send(es.at[:, rows], er.at[:, rows], e_ss.at[k], e_rs.at[k], partner)
 
+    def hop(src, dst, sems, k, q, dev):
+        rows = chain_rows(k)
+        return send(src.at[q, rows], dst.at[q, rows], sems[0].at[k, q], sems[1].at[k, q], dev)
+
+    def d_copy(k, q):
+        return hop(ds, dr, (d_ss, d_rs), k, q, below)
+
+    def l_copy(k, q):
+        return hop(ls, lr, (l_ss, l_rs), k, q, below)
+
     def u_copy(k, q):
-        rows = chain_rows(k)
-        return send(us.at[q, rows], ur.at[q, rows], u_ss.at[k, q], u_rs.at[k, q], below)
-
-    def m_copy(k, q, ref):
-        rows = chain_rows(k)
-        return send(ref.at[q, rows], mr.at[q, rows], m_ss.at[k, q], m_rs.at[k, q], partner)
+        return hop(us, ur, (u_ss, u_rs), k, q, above)
+
+    def u_pass(k, q):
+        return hop(ur, ur, (u_ss, u_rs), k, q, above)
+
+    def m_copy(k, q):
+        return hop(ms, mr, (m_ss, m_rs), k, q, partner)
 
     def og_copy(k):
         rows = chain_rows(k)
@@ -309,17 +331,11 @@
             for b in range(4)
         ]
 
-    def finish(k):
-        rows = chain_rows(k)
-        for q in range(2):
-            m_copy(k, q, us).wait_recv()
-            b = (1 - c) * 2 + q
-            m = mr[q, rows, :].astype(F32)
-            out[b, rows, :] = jnp.where(c == 1, m + own[b, rows, :], m).astype(BF16)
-        for cp in og_copy(k):
-            cp.start()
-
-    def chain_step(k, first):
+    def pair_sum(k, q):
+        rows = chain_rows(k)
+        return own[c * 2 + q, rows, :] + er[q, rows, :].astype(F32)
+
+    def own_step(k):
         rows = chain_rows(k)
         acc = jnp.zeros((CH, 1), F32)
         for b in range(4):
@@ -335,57 +351,124 @@
         for q in range(2):
             es[q, rows, :] = own[(1 - c) * 2 + q, rows, :].astype(BF16)
         e_copy(k).start()
-        e_copy(k).wait_recv()
+
+    def when_step(t, lag, role, fn):
+        k = t - lag
+
+        @pl.when(role & (k >= 0) & (k < NCH))
+        def _():
+            fn(k)
+
+    def down_step(k):
+        rows = chain_rows(k)
         for q in range(2):
 
             @pl.when(z < 7)
             def _():
+                d_copy(k, q).wait_recv()
+
+            @pl.when(z > 2)
+            def _():
+                ds[q, rows, :] = (dr[q, rows, :].astype(F32) + pair_sum(k, q)).astype(BF16)
+                d_copy(k, q).start()
+
+    def low_step(k):
+        rows = chain_rows(k)
+        for q in range(2):
+
+            @pl.when(z < 3)
+            def _():
+                l_copy(k, q).wait_recv()
+
+            @pl.when(z > 0)
+            def _():
+                ls[q, rows, :] = (lr[q, rows, :].astype(F32) + pair_sum(k, q)).astype(BF16)
+                l_copy(k, q).start()
+
+    def up_step(k):
+        rows = chain_rows(k)
+        for q in range(2):
+
+            @pl.when(z != 4)
+            def _():
                 u_copy(k, q).wait_recv()
 
+            @pl.when(z >= 4)
+            def _():
+                us[q, rows, :] = (ur[q, rows, :].astype(F32) + pair_sum(k, q)).astype(BF16)
+                u_copy(k, q).start()
+
+            @pl.when(z == 0)
+            def _():
+                u_pass(k, q).start()
+
+    def final_step(k):
+        rows = chain_rows(k)
+
+        def finish(q, u):
             b = c * 2 + q
-            u = ur[q, rows, :].astype(F32)
             mine = u + own[b, rows, :]
-            un = mine + er[q, rows, :].astype(F32)
-            unb = un.astype(BF16)
-            us[q, rows, :] = unb
-
-            @pl.when(z > 0)
-            def _():
-                u_copy(k, q).start()
-
-            @pl.when(c == 0)
-            def _():
-                m_copy(k, q, ur).start()
-
-            @pl.when(c == 1)
-            def _():
-                m_copy(k, q, us).start()
-
-            out[b, rows, :] = jnp.where(c == 1, mine.astype(BF16), unb)
-
-        if not first:
-            finish(k - 1)
-
-    fwd_slot = jnp.where(z == 7, 1, 0)
-    upd_slot = jnp.minimum(z, 4)
-
-    for i in range(NMB + 1):
-
-        @pl.when(fwd_slot == i)
+            both = mine + er[q, rows, :].astype(F32)
+            ms[q, rows, :] = jnp.where(c == 0, u, both).astype(BF16)
+            m_copy(k, q).start()
+            out[b, rows, :] = jnp.where(c == 0, both, mine).astype(BF16)
+
+        for q in range(2):
+
+            @pl.when(z >= 2)
+            def _():
+                finish(q, dr[q, rows, :].astype(F32))
+
+            @pl.when(z < 2)
+            def _():
+                finish(q, ur[q, rows, :].astype(F32) + lr[q, rows, :].astype(F32))
+
+    def other_step(k):
+        rows = chain_rows(k)
+        for q in range(2):
+            m_copy(k, q).wait_recv()
+            b = (1 - c) * 2 + q
+            m = mr[q, rows, :].astype(F32)
+            out[b, rows, :] = jnp.where(c == 1, m + own[b, rows, :], m).astype(BF16)
+        for cp in og_copy(k):
+            cp.start()
+
+    up_lag = 1 + HOP * jnp.where(z >= 4, z - 4, 4 + z)
+    down_lag = 1 + HOP * (7 - z)
+    low_lag = 1 + HOP * (3 - z)
+    final_lag = jnp.where(z >= 2, down_lag, up_lag)
+
+    def slot(t, carry):
+        @pl.when(t < NCH)
+        def _():
+            @pl.when(t % 2 == 0)
+            def _():
+                for n in range(3):
+                    s_recv(t // 2, n).wait_recv()
+
+            own_step(t)
+
+        @pl.when((t >= 1) & (t <= NCH))
+        def _():
+            e_copy(t - 1).wait_recv()
+
+        when_step(t, low_lag, z <= 3, low_step)
+        when_step(t, up_lag, (z >= 4) | (z <= 1), up_step)
+        when_step(t, down_lag, z >= 2, down_step)
+        when_step(t, final_lag, z >= 0, final_step)
+        when_step(t, final_lag + 1, z >= 0, other_step)
+
+        @pl.when(t == FORWARD_SLOT)
         def _():
             reduce_forward()
 
-        @pl.when(upd_slot == i)
+        @pl.when(t == UPDATE_SLOT)
         def _():
             update()
 
-        if i < NMB:
-            for n in range(3):
-                sr_out[i * 3 + n].wait_recv()
-            for h in range(MB // CH):
-                k = i * (MB // CH) + h
-                chain_step(k, k == 0)
-    finish(NCH - 1)
+        return carry
+
+    lax.fori_loop(0, NCH + 2 + 5 * HOP, slot, 0)
 
     for cp in r_out:
         cp.wait_recv()
@@ -399,9 +482,17 @@
     def drain(k, carry):
         e_copy(k).wait_send()
         for q in range(2):
-            m_copy(k, q, us).wait_send()
-
-            @pl.when(z > 0)
+            m_copy(k, q).wait_send()
+
+            @pl.when(z > 2)
+            def _():
+                d_copy(k, q).wait_send()
+
+            @pl.when((z > 0) & (z < 4))
+            def _():
+                l_copy(k, q).wait_send()
+
+            @pl.when((z >= 4) | (z == 0))
             def _():
                 u_copy(k, q).wait_send()
 
@@ -413,6 +504,24 @@
     mn_copy.wait()
     sn_copy.wait()
     ro_copy.wait()
+
+
+def land(*refs):
+    srcs, dsts, bufs, (in_sem, out_sem) = refs[:4], refs[4:8], refs[8:12], refs[12:]
+    ins, outs = [], []
+    for i in range(4):
+        rows = srcs[i].shape[0] // LAND
+        for j in range(LAND):
+            part = pl.ds(j * rows, rows)
+            ins.append(pltpu.make_async_copy(srcs[i].at[part], bufs[i].at[part], in_sem.at[i, j]))
+            outs.append(pltpu.make_async_copy(bufs[i].at[part], dsts[i].at[part], out_sem.at[i, j]))
+    for cp in ins:
+        cp.start()
+    for cp, nxt in zip(ins, outs):
+        cp.wait()
+        nxt.start()
+    for cp in outs:
+        cp.wait()
 
 
 def shards(tokens, cotangents, norm_gain, master, moment, second, head_owner, plan):
@@ -428,12 +537,11 @@
         V((4 * R, C), F32), V((R, C), BF16), V((R, C), BF16), V((R, C), BF16),
         V((H, C), BF16), V((H, C), BF16), V((R, C), BF16), V((R, C), BF16),
         V((R, C), BF16), V((16, RO, R), BF16), V((16, RO, R), BF16), V((RO, D), BF16),
-        V((4, T, QD), F32), V((2, T, QD), BF16), V((2, T, QD), BF16), V((2, T, QD), BF16),
-        V((2, T, QD), BF16), V((2, T, QD), BF16), V((4, T, QD), BF16),
+        V((4, T, QD), F32), *[V((2, T, QD), BF16) for _ in range(10)], V((4, T, QD), BF16),
         dma((5,)), dma((3,)), dma((NCH, 4)),
         dma((6,)), dma((6,)), dma((6,)), dma((6,)), dma((3,)), dma((3,)),
         dma((NMB, 3)), dma((NMB, 3)), dma((6,)), dma((6,)), dma((15,)), dma((15,)),
-        dma((NCH,)), dma((NCH,)), dma((NCH, 2)), dma((NCH, 2)), dma((NCH, 2)), dma((NCH, 2)),
+        dma((NCH,)), dma((NCH,)), *[dma((NCH, 2)) for _ in range(8)],
     ]
     ig, mn, sn, ro = pl.pallas_call(
         kernel,
@@ -454,7 +562,16 @@
             collective_id=0, has_side_effects=True, vmem_limit_bytes=56 * 1024 * 1024
         ),
     )(tokens[0], cotangents[0], norm_gain, master[0], moment[0], second[0], head_owner[0], plan)
-    return (ig[None], mn[None], sn[None], ro[None])
+    outs = (ig, mn, sn, ro)
+    outs = pl.pallas_call(
+        land,
+        out_shape=tuple(jax.ShapeDtypeStruct(v.shape, v.dtype) for v in outs),
+        in_specs=[hbm] * 4,
+        out_specs=(hbm,) * 4,
+        scratch_shapes=[V(v.shape, v.dtype) for v in outs] + [dma((4, LAND)), dma((4, LAND))],
+        name="land",
+    )(*outs)
+    return tuple(v[None] for v in outs)
 
 
 def solution(mesh):

time: 101 us -> 86.3 us (0.85)
  Pallas kernels: 93 us -> 84.1 us
  local copies, waits for them, and re-layouts: 6.72 us -> 0 us
    pallas_call x1, Pallas kernels: 93 us -> 80.6 us  [shards(): pl.pallas_call(kernel, out_shape=(jax.ShapeDtypeStruct((T, D), BF16), jax...]
    unnamed x10 -> x0, local copies, waits for them, and re-layouts: 6.72 us -> none
    pallas_call x0 -> x1, Pallas kernels: none -> 3.52 us  [shards(): pl.pallas_call(land, out_shape=tuple((jax.ShapeDtypeStruct(v.shape, v.dty...]
where the time goes in v2:
time: 86.3 us; the launch traced here: 84.7 us
  Pallas kernels  84.1 us (97%)
    pallas_call x1, Pallas kernels, shards(): pl.pallas_call(kernel, out_shape=(jax.ShapeDtypeStruct((T, D), BF16), jax...  80.6 us
    pallas_call x1, Pallas kernels, shards(): pl.pallas_call(land, out_shape=tuple((jax.ShapeDtypeStruct(v.shape, v.dty...  3.52 us

profile of v2, /device:TPU:1, one launch (start us, length us, event | category | flops | bytes accessed | tf_op | source)
XLA Modules:
  0.0 84.7 jit_solution(13381429041499158495)
XLA Ops:
  0.6 80.6 %layer_backward.1 = (bf16[128,5120]{1,0:T(8,128)(2,1)}, f32[320,1024]{1,0:T(8,128)}, f32[320,1024]{1,0:T(8,128)}, bf16[64,5120]{1,0:T(8,128)(2,1)}) custom-call(bf16[128,5120]{1,0:T(8,128)(2,1)} %bitcast.10, bf16[128,1024]{1,0:T(8,128)(2,1)} %bitcast.18, f32[1,5120]{1,0:T(1,128)} %gain.1, f32[320,1024]{1,0:T(8,128)} %bitcast.11, f32[320,1024]{1,0:T(8,128)} %bitcast.12, ...), custom_call_target="tpu_custom_call" | custom-call | flops 2684354560 | bytes 12000000 | tf_op jit(solution)/shard_map/layer_backward/pallas_call | solution.py:546
  81.2 3.5 %land.1 = (bf16[128,5120]{1,0:T(8,128)(2,1)}, f32[320,1024]{1,0:T(8,128)}, f32[320,1024]{1,0:T(8,128)}, bf16[64,5120]{1,0:T(8,128)(2,1)}) custom-call(bf16[128,5120]{1,0:T(8,128)(2,1)} %get-tuple-element.12.refs_0_, f32[320,1024]{1,0:T(8,128)} %get-tuple-element.13.refs_1_, f32[320,1024]{1,0:T(8,128)} %get-tuple-element.14.refs_2_, ...), custom_call_target="tpu_custom_call" | custom-call | tf_op jit(solution)/shard_map/land/pallas_call | solution.py:566

commit v3 on v2

--- a/solution.py
+++ b/solution.py
@@ -1,5 +1,3 @@
-import functools
-
 import jax
 import jax.numpy as jnp
 from jax import lax
@@ -26,14 +24,21 @@
 R = 320
 H = R // 2
 QD = D // 4
-HD = D // 2
 MB = 32
 NMB = 4
 CH = 16
 NCH = T // CH
 HOP = 2
 FORWARD_SLOT = 4
-UPDATE_SLOT = 10
+UPDATE_SLOT = 11
+UROWS = 160
+HEADS = 2
+DIRECT_SLOT = 2
+ROLLOUT_SLOT = 20
+OPPOSITE_AFTER = 1
+REST_AFTER = 2
+BASE = 2
+BACK = 2
 LAND = 1
 RO = 64
 
@@ -76,7 +81,7 @@
             [(mas_hbm, mas), (cot_hbm, cot), (tok_hbm, tok), (mom_hbm, mom), (sec_hbm, sec)]
         )
     ]
-    for ld in loads:
+    for ld in loads[:2]:
         ld.start()
 
     bar = pltpu.get_barrier_semaphore()
@@ -90,6 +95,9 @@
         @pl.when(z == top)
         def _():
             ref[...] = jnp.zeros_like(ref)
+
+    for ld in loads[2:]:
+        ld.start()
 
     def w_rows(block, half):
         return pl.ds(pl.multiple_of(block * R + half * H, 32), H)
@@ -111,7 +119,7 @@
     for n, (dev, half) in enumerate([(1, 0), (3, 1), (1, 1), (3, 0)]):
         rows = w_rows(x, half)
         w_out.append(send(wg.at[rows], wg.at[rows], w_ss.at[n], w_rs.at[n], at_x(dev)))
-    for cp in w_out:
+    for cp in w_out[:2]:
         cp.start()
 
     g_out = []
@@ -148,6 +156,10 @@
         cp.start()
     xr[0] = xs[y]
 
+    for first, second in zip(w_out[:2], w_out[2:]):
+        first.wait_send()
+        second.start()
+
     g_out[0].wait_recv()
     rows0, rows1 = pl.ds(0, hg), pl.ds(hg, hg)
     g_fwd = [send(g.at[1, rows0], g.at[2, rows0], g_ss.at[4], g_rs.at[4], at_y(1))]
@@ -169,50 +181,13 @@
         cp.wait_recv()
     proj_scale = D ** (-0.5)
 
-    for cp in x_out:
-        cp.wait_recv()
-    gall = g[...].reshape(4 * T, C)
-    for q in range(5):
-        lhs = jnp.concatenate([xr[r, :, q * 256 : (q + 1) * 256] for r in range(4)], axis=0)
-        pf[q * 256 : (q + 1) * 256, :] = (
-            lax.dot_general(lhs, gall, (((0,), (0,)), ((), ())), preferred_element_type=F32)
-            * proj_scale
-        )
-
-    def p_rows(d, half):
-        return pf[pl.ds(pl.multiple_of(lax.rem(x + d, 4) * R + half * H, 32), H), :]
-
-    s_opp[0:H, :] = p_rows(2, 0).astype(BF16)
-    s_opp[H:R, :] = p_rows(2, 1).astype(BF16)
-    p_out = [
-        send(s_opp.at[pl.ds(0, H)], o_left, p_ss.at[0], p_rs.at[0], at_x(1)),
-        send(s_opp.at[pl.ds(H, H)], o_right, p_ss.at[1], p_rs.at[1], at_x(3)),
-    ]
-    for cp in p_out:
-        cp.start()
-    s_right[H:R, :] = p_rows(1, 1).astype(BF16)
-    s_left[0:H, :] = p_rows(3, 0).astype(BF16)
-    p_out += [
-        send(s_right.at[pl.ds(H, H)], r_left.at[pl.ds(H, H)], p_ss.at[2], p_rs.at[2], at_x(1)),
-        send(s_left.at[pl.ds(0, H)], r_right.at[pl.ds(0, H)], p_ss.at[3], p_rs.at[3], at_x(3)),
-    ]
-    for cp in p_out[2:]:
-        cp.start()
-    p_out += [
-        send(s_right.at[pl.ds(0, H)], r_left.at[pl.ds(0, H)], p_ss.at[4], p_rs.at[4], at_x(1)),
-        send(s_left.at[pl.ds(H, H)], r_right.at[pl.ds(H, H)], p_ss.at[5], p_rs.at[5], at_x(3)),
-    ]
-
-    for cp in (w_out[2], w_out[3], w_fwd[0], w_fwd[1]):
-        cp.wait_recv()
-
     sr_out = []
 
     def s_recv(i, n):
         rows = pl.ds(pl.multiple_of(i * MB, MB), MB)
         return send(ss.at[0, rows], sr.at[0, rows], s_ss.at[i, n], s_rs.at[i, n], at_y(1))
 
-    for i in range(NMB):
+    def spread_block(i):
         rows = pl.ds(i * MB, MB)
         lhs = jnp.concatenate([g[r, i * MB : (i + 1) * MB, :] for r in range(4)], axis=0)
         for q in range(5):
@@ -232,6 +207,60 @@
             cp.start()
             sr_out.append(cp)
 
+    def gradient_block(i):
+        q = lax.rem(lax.rem(x + 2, 4) + i, 5)
+        cols = pl.ds(pl.multiple_of(q * 256, 256), 256)
+        lhs = jnp.concatenate([xr[r, :, cols] for r in range(4)], axis=0)
+        pf[cols, :] = (
+            lax.dot_general(
+                lhs, g[...].reshape(4 * T, C), (((0,), (0,)), ((), ())),
+                preferred_element_type=F32,
+            )
+            * proj_scale
+        )
+
+    def p_rows(d, half):
+        return pf[pl.ds(pl.multiple_of(lax.rem(x + d, 4) * R + half * H, 32), H), :]
+
+    p_out = [
+        send(s_opp.at[pl.ds(0, H)], o_left, p_ss.at[0], p_rs.at[0], at_x(1)),
+        send(s_opp.at[pl.ds(H, H)], o_right, p_ss.at[1], p_rs.at[1], at_x(3)),
+        send(s_right.at[pl.ds(H, H)], r_left.at[pl.ds(H, H)], p_ss.at[2], p_rs.at[2], at_x(1)),
+        send(s_left.at[pl.ds(0, H)], r_right.at[pl.ds(0, H)], p_ss.at[3], p_rs.at[3], at_x(3)),
+        send(s_right.at[pl.ds(0, H)], r_left.at[pl.ds(0, H)], p_ss.at[4], p_rs.at[4], at_x(1)),
+        send(s_left.at[pl.ds(H, H)], r_right.at[pl.ds(H, H)], p_ss.at[5], p_rs.at[5], at_x(3)),
+    ]
+
+    def gradient_opposite():
+        for cp in x_out:
+            cp.wait_recv()
+        for i in range(2):
+            gradient_block(i)
+        s_opp[0:H, :] = p_rows(2, 0).astype(BF16)
+        s_opp[H:R, :] = p_rows(2, 1).astype(BF16)
+        for cp in p_out[:2]:
+            cp.start()
+
+    def gradient_rest():
+        for i in range(2, 5):
+            gradient_block(i)
+        s_right[H:R, :] = p_rows(1, 1).astype(BF16)
+        s_left[0:H, :] = p_rows(3, 0).astype(BF16)
+
+    for cp in (w_out[2], w_out[3], w_fwd[0], w_fwd[1]):
+        cp.wait_recv()
+    for i in range(NMB):
+        spread_block(i)
+        if i == OPPOSITE_AFTER:
+            gradient_opposite()
+        if i == REST_AFTER:
+            gradient_rest()
+
+    def reduce_direct():
+        for first, second in zip(p_out[:2], p_out[2:4]):
+            first.wait_send()
+            second.start()
+
     def reduce_forward():
         p_out[0].wait_recv()
         s_right[0:H, :] = (p_rows(1, 0) + o_left[...].astype(F32)).astype(BF16)
@@ -244,24 +273,24 @@
     sn_copy = pltpu.make_async_copy(sec, sn_hbm, out_sem.at[1])
     ro_copy = pltpu.make_async_copy(ro, ro_hbm, out_sem.at[2])
 
-    r_out = [
-        send(
-            rs.at[lax.rem(f + k, 16)], rr.at[f], r_ss.at[k - 1], r_rs.at[k - 1],
-            (s, lax.rem(f + k, 16)),
-        )
-        for k in range(1, 16)
-    ]
-
-    def update():
+    def r_send(dest):
+        return send(rs.at[dest], rr.at[f], r_ss.at[dest], r_rs.at[f], (s, dest))
+
+    def r_recv(src):
+        return send(rs.at[src], rr.at[src], r_ss.at[src], r_rs.at[src], (s, src))
+
+    def update_wait():
         for cp in p_out[2:]:
             cp.wait_recv()
         loads[3].wait()
         loads[4].wait()
 
+    def update_rows(u):
         def adam(k, carry):
-            rows = pl.ds(pl.multiple_of(k * 32, 32), 32)
+            row = u * UROWS + k * 32
+            rows = pl.ds(pl.multiple_of(row, 32), 32)
             grad = (
-                pf[pl.ds(pl.multiple_of(x * R + k * 32, 32), 32), :]
+                pf[pl.ds(pl.multiple_of(x * R + row, 32), 32), :]
                 + r_left[rows, :].astype(F32)
                 + r_right[rows, :].astype(F32)
             )
@@ -274,27 +303,27 @@
             wnew[rows, :] = (old - learn_rate * (step + weight_decay * old)).astype(BF16)
             return carry
 
-        lax.fori_loop(0, R // 32, adam, 0)
-        mn_copy.start()
-        sn_copy.start()
-
+        lax.fori_loop(0, UROWS // 32, adam, 0)
+
+    def rollout_head(j):
         ia = lax.broadcasted_iota(jnp.int32, (128, 128), 0)
         ib = lax.broadcasted_iota(jnp.int32, (128, 128), 1)
         eye = jnp.where(ia == ib, 1.0, 0.0).astype(BF16)
-        for j in range(4):
-            o = owner[j]
-            for p in range(2):
-                v = wnew[:, p * 512 : p * 512 + 128]
-                for h in range(1, 4):
-                    v = jnp.where(o == h, wnew[:, p * 512 + h * 128 : p * 512 + (h + 1) * 128], v)
-                t = lax.dot_general(
-                    eye, v, (((1,), (1,)), ((), ())), preferred_element_type=F32
-                ).astype(BF16)
-                rs[j * 4 + p * 2] = t[0:RO]
-                rs[j * 4 + p * 2 + 1] = t[RO : 2 * RO]
-        for cp in r_out:
-            cp.start()
-        rr[f] = rs[f]
+        o = owner[j]
+        for p in range(2):
+            v = wnew[:, p * 512 : p * 512 + 128]
+            for h in range(1, 4):
+                v = jnp.where(o == h, wnew[:, p * 512 + h * 128 : p * 512 + (h + 1) * 128], v)
+            t = lax.dot_general(
+                eye, v, (((1,), (1,)), ((), ())), preferred_element_type=F32
+            ).astype(BF16)
+            for half in range(2):
+                dest = j * 4 + p * 2 + half
+                rs[dest] = t[half * RO : (half + 1) * RO]
+
+                @pl.when(dest != f)
+                def _():
+                    r_send(dest).start()
 
     def chain_rows(k):
         return pl.ds(pl.multiple_of(k * CH, CH), CH)
@@ -319,17 +348,18 @@
     def u_pass(k, q):
         return hop(ur, ur, (u_ss, u_rs), k, q, above)
 
-    def m_copy(k, q):
-        return hop(ms, mr, (m_ss, m_rs), k, q, partner)
+    def m_copy(k):
+        rows = pl.ds(pl.multiple_of((k // 2) * 2 * CH, 2 * CH), 2 * CH)
+        return send(
+            ms.at[:, rows], mr.at[:, rows], m_ss.at[k // 2], m_rs.at[k // 2], partner
+        )
 
     def og_copy(k):
-        rows = chain_rows(k)
-        return [
-            pltpu.make_async_copy(
-                out.at[b, rows], ig_hbm.at[rows, pl.ds(b * QD, QD)], og_sem.at[k, b]
-            )
-            for b in range(4)
-        ]
+        rows = pl.ds(pl.multiple_of((k // 2) * 2 * CH, 2 * CH), 2 * CH)
+        return pltpu.make_async_copy(out.at[rows], ig_hbm.at[rows], og_sem.at[k // 2])
+
+    def quarter(b):
+        return pl.ds(pl.multiple_of(b * QD, QD), QD)
 
     def pair_sum(k, q):
         rows = chain_rows(k)
@@ -410,32 +440,36 @@
             mine = u + own[b, rows, :]
             both = mine + er[q, rows, :].astype(F32)
             ms[q, rows, :] = jnp.where(c == 0, u, both).astype(BF16)
-            m_copy(k, q).start()
-            out[b, rows, :] = jnp.where(c == 0, both, mine).astype(BF16)
-
-        for q in range(2):
-
-            @pl.when(z >= 2)
-            def _():
+            out[rows, quarter(b)] = jnp.where(c == 0, both, mine).astype(BF16)
+
+        @pl.when(z >= 2)
+        def _():
+            for q in range(2):
                 finish(q, dr[q, rows, :].astype(F32))
 
-            @pl.when(z < 2)
-            def _():
+        @pl.when(z < 2)
+        def _():
+            for q in range(2):
                 finish(q, ur[q, rows, :].astype(F32) + lr[q, rows, :].astype(F32))
 
+        @pl.when(k % 2 == 1)
+        def _():
+            m_copy(k).start()
+
     def other_step(k):
-        rows = chain_rows(k)
-        for q in range(2):
-            m_copy(k, q).wait_recv()
-            b = (1 - c) * 2 + q
-            m = mr[q, rows, :].astype(F32)
-            out[b, rows, :] = jnp.where(c == 1, m + own[b, rows, :], m).astype(BF16)
-        for cp in og_copy(k):
-            cp.start()
-
-    up_lag = 1 + HOP * jnp.where(z >= 4, z - 4, 4 + z)
-    down_lag = 1 + HOP * (7 - z)
-    low_lag = 1 + HOP * (3 - z)
+        @pl.when(k % 2 == 1)
+        def _():
+            rows = pl.ds(pl.multiple_of((k // 2) * 2 * CH, 2 * CH), 2 * CH)
+            m_copy(k).wait_recv()
+            for q in range(2):
+                b = (1 - c) * 2 + q
+                m = mr[q, rows, :].astype(F32)
+                out[rows, quarter(b)] = jnp.where(c == 1, m + own[b, rows, :], m).astype(BF16)
+            og_copy(k).start()
+
+    up_lag = BASE + HOP * jnp.where(z >= 4, z - 4, 4 + z)
+    down_lag = BASE + HOP * (7 - z)
+    low_lag = BASE + HOP * (3 - z)
     final_lag = jnp.where(z >= 2, down_lag, up_lag)
 
     def slot(t, carry):
@@ -448,41 +482,75 @@
 
             own_step(t)
 
-        @pl.when((t >= 1) & (t <= NCH))
-        def _():
-            e_copy(t - 1).wait_recv()
+        @pl.when((t >= BASE) & (t < NCH + BASE))
+        def _():
+            e_copy(t - BASE).wait_recv()
 
         when_step(t, low_lag, z <= 3, low_step)
         when_step(t, up_lag, (z >= 4) | (z <= 1), up_step)
         when_step(t, down_lag, z >= 2, down_step)
         when_step(t, final_lag, z >= 0, final_step)
-        when_step(t, final_lag + 1, z >= 0, other_step)
+        when_step(t, final_lag + BACK, z >= 0, other_step)
+
+        @pl.when(t == DIRECT_SLOT)
+        def _():
+            reduce_direct()
 
         @pl.when(t == FORWARD_SLOT)
         def _():
             reduce_forward()
 
-        @pl.when(t == UPDATE_SLOT)
-        def _():
-            update()
+        u = t - UPDATE_SLOT
+
+        @pl.when(u == 0)
+        def _():
+            update_wait()
+
+        @pl.when((u >= 0) & (u < R // UROWS))
+        def _():
+            update_rows(u)
+
+        @pl.when(u == R // UROWS)
+        def _():
+            mn_copy.start()
+            sn_copy.start()
+
+        j = u - R // UROWS
+
+        @pl.when((j >= 0) & (j < 4 // HEADS))
+        def _():
+            for n in range(HEADS):
+                rollout_head(j * HEADS + n)
+
+        @pl.when(t == ROLLOUT_SLOT)
+        def _():
+            rr[f] = rs[f]
+            for k in range(1, 16):
+                r_recv(lax.rem(f + k, 16)).wait_recv()
+            for i in range(8):
+                ro[:, i * 2 * R : (i + 1) * 2 * R] = jnp.concatenate(
+                    [rr[2 * i], rr[2 * i + 1]], axis=1
+                )
+            ro_copy.start()
 
         return carry
 
-    lax.fori_loop(0, NCH + 2 + 5 * HOP, slot, 0)
-
-    for cp in r_out:
-        cp.wait_recv()
-    for i in range(8):
-        ro[:, i * 2 * R : (i + 1) * 2 * R] = jnp.concatenate([rr[2 * i], rr[2 * i + 1]], axis=1)
-    ro_copy.start()
-
-    for cp in w_out + w_fwd + g_out + g_fwd + x_out + sr_out + p_out + r_out:
+    lax.fori_loop(0, NCH + BASE + BACK + 5 * HOP, slot, 0)
+
+    for cp in w_out[2:] + w_fwd + g_out + g_fwd + x_out + sr_out + p_out[2:]:
         cp.wait_send()
+    for k in range(1, 16):
+        r_send(lax.rem(f + k, 16)).wait_send()
 
     def drain(k, carry):
         e_copy(k).wait_send()
+
+        @pl.when(k % 2 == 1)
+        def _():
+            m_copy(k).wait_send()
+            og_copy(k).wait()
+
         for q in range(2):
-            m_copy(k, q).wait_send()
 
             @pl.when(z > 2)
             def _():
@@ -496,8 +564,6 @@
             def _():
                 u_copy(k, q).wait_send()
 
-        for cp in og_copy(k):
-            cp.wait()
         return carry
 
     lax.fori_loop(0, NCH, drain, 0)
@@ -537,11 +603,12 @@
         V((4 * R, C), F32), V((R, C), BF16), V((R, C), BF16), V((R, C), BF16),
         V((H, C), BF16), V((H, C), BF16), V((R, C), BF16), V((R, C), BF16),
         V((R, C), BF16), V((16, RO, R), BF16), V((16, RO, R), BF16), V((RO, D), BF16),
-        V((4, T, QD), F32), *[V((2, T, QD), BF16) for _ in range(10)], V((4, T, QD), BF16),
-        dma((5,)), dma((3,)), dma((NCH, 4)),
+        V((4, T, QD), F32), *[V((2, T, QD), BF16) for _ in range(10)], V((T, D), BF16),
+        dma((5,)), dma((3,)), dma((NCH,)),
         dma((6,)), dma((6,)), dma((6,)), dma((6,)), dma((3,)), dma((3,)),
-        dma((NMB, 3)), dma((NMB, 3)), dma((6,)), dma((6,)), dma((15,)), dma((15,)),
-        dma((NCH,)), dma((NCH,)), *[dma((NCH, 2)) for _ in range(8)],
+        dma((NMB, 3)), dma((NMB, 3)), dma((6,)), dma((6,)), dma((16,)), dma((16,)),
+        dma((NCH,)), dma((NCH,)), *[dma((NCH, 2)) for _ in range(6)],
+        dma((NCH,)), dma((NCH,)),
     ]
     ig, mn, sn, ro = pl.pallas_call(
         kernel,

time: 86.3 us -> 83.9 us (0.972); the launches traced: 84.7 us -> 83.4 us
  Pallas kernels: 84.1 us -> 82.8 us
    pallas_call x1, Pallas kernels: 80.6 us -> 79.3 us  [shards(): pl.pallas_call(kernel, out_shape=(jax.ShapeDtypeStruct((T, D), BF16), jax...]
where the time goes in v3:
time: 83.9 us; the launch traced here: 83.4 us
  Pallas kernels  82.8 us (99%)
    pallas_call x1, Pallas kernels, shards(): pl.pallas_call(kernel, out_shape=(jax.ShapeDtypeStruct((T, D), BF16), jax...  79.3 us
    pallas_call x1, Pallas kernels, shards(): pl.pallas_call(land, out_shape=tuple((jax.ShapeDtypeStruct(v.shape, v.dty...  3.52 us

profile of v3, /device:TPU:1, one launch (start us, length us, event | category | flops | bytes accessed | tf_op | source)
XLA Modules:
  0.0 83.4 jit_solution(13935152525906825156)
XLA Ops:
  0.6 79.3 %layer_backward.1 = (bf16[128,5120]{1,0:T(8,128)(2,1)}, f32[320,1024]{1,0:T(8,128)}, f32[320,1024]{1,0:T(8,128)}, bf16[64,5120]{1,0:T(8,128)(2,1)}) custom-call(bf16[128,5120]{1,0:T(8,128)(2,1)} %bitcast.10, bf16[128,1024]{1,0:T(8,128)(2,1)} %bitcast.18, f32[1,5120]{1,0:T(1,128)} %gain.1, f32[320,1024]{1,0:T(8,128)} %bitcast.11, f32[320,1024]{1,0:T(8,128)} %bitcast.12, ...), custom_call_target="tpu_custom_call" | custom-call | flops 2684354560 | bytes 12000000 | tf_op jit(solution)/shard_map/layer_backward/pallas_call | solution.py:613
  79.9 3.5 %land.1 = (bf16[128,5120]{1,0:T(8,128)(2,1)}, f32[320,1024]{1,0:T(8,128)}, f32[320,1024]{1,0:T(8,128)}, bf16[64,5120]{1,0:T(8,128)(2,1)}) custom-call(bf16[128,5120]{1,0:T(8,128)(2,1)} %get-tuple-element.12.refs_0_, f32[320,1024]{1,0:T(8,128)} %get-tuple-element.13.refs_1_, f32[320,1024]{1,0:T(8,128)} %get-tuple-element.14.refs_2_, ...), custom_call_target="tpu_custom_call" | custom-call | tf_op jit(solution)/shard_map/land/pallas_call | solution.py:633

commit v4 on v3

--- a/solution.py
+++ b/solution.py
@@ -35,8 +35,6 @@
 HEADS = 2
 DIRECT_SLOT = 2
 ROLLOUT_SLOT = 20
-OPPOSITE_AFTER = 1
-REST_AFTER = 2
 BASE = 2
 BACK = 2
 LAND = 1
@@ -187,9 +185,9 @@
         rows = pl.ds(pl.multiple_of(i * MB, MB), MB)
         return send(ss.at[0, rows], sr.at[0, rows], s_ss.at[i, n], s_rs.at[i, n], at_y(1))
 
-    def spread_block(i):
-        rows = pl.ds(i * MB, MB)
-        lhs = jnp.concatenate([g[r, i * MB : (i + 1) * MB, :] for r in range(4)], axis=0)
+    def spread_pair(i):
+        first = i * 2 * MB
+        lhs = jnp.concatenate([g[r, first : first + 2 * MB, :] for r in range(4)], axis=0)
         for q in range(5):
             cols = slice(q * 256, (q + 1) * 256)
             v = (
@@ -200,12 +198,16 @@
                 * proj_scale
             ).astype(BF16)
             for r in range(1, 4):
-                ss[r, i * MB : (i + 1) * MB, cols] = v[r * MB : (r + 1) * MB]
-            sr[y, i * MB : (i + 1) * MB, cols] = v[0:MB]
-        for n, r in enumerate([2, 1, 3]):
-            cp = send(ss.at[r, rows], sr.at[y, rows], s_ss.at[i, n], s_rs.at[i, n], at_y(4 - r))
-            cp.start()
-            sr_out.append(cp)
+                ss[r, first : first + 2 * MB, cols] = v[r * 2 * MB : (r + 1) * 2 * MB]
+            sr[y, first : first + 2 * MB, cols] = v[0 : 2 * MB]
+        for m in (2 * i, 2 * i + 1):
+            rows = pl.ds(m * MB, MB)
+            for n, r in enumerate([2, 1, 3]):
+                cp = send(
+                    ss.at[r, rows], sr.at[y, rows], s_ss.at[m, n], s_rs.at[m, n], at_y(4 - r)
+                )
+                cp.start()
+                sr_out.append(cp)
 
     def gradient_block(i):
         q = lax.rem(lax.rem(x + 2, 4) + i, 5)
@@ -249,12 +251,10 @@
 
     for cp in (w_out[2], w_out[3], w_fwd[0], w_fwd[1]):
         cp.wait_recv()
-    for i in range(NMB):
-        spread_block(i)
-        if i == OPPOSITE_AFTER:
-            gradient_opposite()
-        if i == REST_AFTER:
-            gradient_rest()
+    spread_pair(0)
+    gradient_opposite()
+    spread_pair(1)
+    gradient_rest()
 
     def reduce_direct():
         for first, second in zip(p_out[:2], p_out[2:4]):

time: 83.9 us -> 83.9 us (level)
  no operation moved by 1% of the time
where the time goes in v4:
time: 83.9 us; the launch traced here: 83.5 us
  Pallas kernels  82.8 us (99%)
    pallas_call x1, Pallas kernels, shards(): pl.pallas_call(kernel, out_shape=(jax.ShapeDtypeStruct((T, D), BF16), jax...  79.3 us
    pallas_call x1, Pallas kernels, shards(): pl.pallas_call(land, out_shape=tuple((jax.ShapeDtypeStruct(v.shape, v.dty...  3.52 us

profile of v4, /device:TPU:1, one launch (start us, length us, event | category | flops | bytes accessed | tf_op | source)
XLA Modules:
  0.0 83.5 jit_solution(3331009177375490101)
XLA Ops:
  0.6 79.3 %layer_backward.1 = (bf16[128,5120]{1,0:T(8,128)(2,1)}, f32[320,1024]{1,0:T(8,128)}, f32[320,1024]{1,0:T(8,128)}, bf16[64,5120]{1,0:T(8,128)(2,1)}) custom-call(bf16[128,5120]{1,0:T(8,128)(2,1)} %bitcast.10, bf16[128,1024]{1,0:T(8,128)(2,1)} %bitcast.18, f32[1,5120]{1,0:T(1,128)} %gain.1, f32[320,1024]{1,0:T(8,128)} %bitcast.11, f32[320,1024]{1,0:T(8,128)} %bitcast.12, ...), custom_call_target="tpu_custom_call" | custom-call | flops 2684354560 | bytes 12000000 | tf_op jit(solution)/shard_map/layer_backward/pallas_call | solution.py:613
  80.0 3.5 %land.1 = (bf16[128,5120]{1,0:T(8,128)(2,1)}, f32[320,1024]{1,0:T(8,128)}, f32[320,1024]{1,0:T(8,128)}, bf16[64,5120]{1,0:T(8,128)(2,1)}) custom-call(bf16[128,5120]{1,0:T(8,128)(2,1)} %get-tuple-element.12.refs_0_, f32[320,1024]{1,0:T(8,128)} %get-tuple-element.13.refs_1_, f32[320,1024]{1,0:T(8,128)} %get-tuple-element.14.refs_2_, ...), custom_call_target="tpu_custom_call" | custom-call | tf_op jit(solution)/shard_map/land/pallas_call | solution.py:633
